TPU v7x, 128 devices: a whole 4x4x4 slice. The times are simulated.
128 devices in a mesh: cent: 16 (over y, z_lo, core), dp: 8 (over x, z_hi).
Axes of the slice: x: 4, y: 4, z: 4 (z_hi: 2, z_lo: 2; z = z_hi * 2 + z_lo), core: 2. Of those that a mesh axis runs over, the one named last changes fastest.
Arguments:
- images: bfloat16 [4096, 1536], P('dp')
- cents: bfloat16 [16384, 1536], P('cent')
- tops: bfloat16 [8192, 1536], P('dp')
Outputs:
- level_one: bfloat16 [16384, 1536], P(('cent', 'dp'))
- level_two: bfloat16 [8, 1024, 1536], P('dp', 'cent')
All inputs are finite; a program needn't handle non-finite values.
Results may differ from a plain program's by a relative error of at most 0.007.
Values may be sent and summed in bfloat16 or wider, within the bound.
A program may use at most 64 MiB of HBM per device.

v0:
```python
import jax
import jax.numpy as jnp
from jax import lax
from jax.sharding import PartitionSpec as P

prior = 0.1


def first_weights(scores):
    local_peak = jnp.max(scores, axis=1)
    peak = lax.pmax(local_peak, "cent")
    expo = jnp.exp(scores - peak[:, None])
    total = lax.psum(jnp.sum(expo, axis=1), "cent")
    return expo / total[:, None]


def second_weights(scores):
    local_peak = jnp.max(scores, axis=1)
    peak = lax.pmax(local_peak, "dp")
    expo = jnp.exp(scores - peak[:, None])
    total = lax.psum(jnp.sum(expo, axis=1), "dp")
    return expo / total[:, None]


def body(images, cents, tops):
    width = images.shape[1]
    scale = width ** (-0.5)
    scores = jnp.einsum("id,kd->ik", images, cents, preferred_element_type=jnp.float32) * scale
    resp = first_weights(scores)
    moved = jnp.einsum(
        "ik,id->kd", resp.astype(jnp.bfloat16), images, preferred_element_type=jnp.float32
    )
    mass = jnp.sum(resp, axis=0)
    share = cents.shape[0] // lax.axis_size("dp")
    offset = lax.axis_index("dp") * share
    moved_all, mass_all = lax.psum((moved, mass), "dp")
    data = ((moved_all + prior * cents.astype(jnp.float32)) / (mass_all + prior)[:, None]).astype(
        jnp.bfloat16
    )
    level_part = lax.dynamic_slice_in_dim(data, offset, share, 0)
    scores_two = jnp.einsum("kd,jd->kj", data, tops, preferred_element_type=jnp.float32) * scale
    resp_two = second_weights(scores_two)
    moved_two = jnp.einsum(
        "kj,kd->jd", resp_two.astype(jnp.bfloat16), data, preferred_element_type=jnp.float32
    )
    mass_two = jnp.sum(resp_two, axis=0)
    moved_top, mass_top = (
        lax.psum_scatter(moved_two, "cent", scatter_dimension=0, tiled=True),
        lax.psum_scatter(mass_two, "cent", scatter_dimension=0, tiled=True),
    )
    top_share = tops.shape[0] // lax.axis_size("cent")
    own_tops = lax.dynamic_slice_in_dim(
        tops, lax.axis_index("cent") * top_share, top_share, 0
    ).astype(jnp.float32)
    level_two = ((moved_top + prior * own_tops) / (mass_top + prior)[:, None]).astype(jnp.bfloat16)
    return (level_part, level_two[None])


def solution(mesh):
    return jax.shard_map(
        body,
        mesh=mesh,
        in_specs=(P("dp", None), P("cent", None), P("dp", None)),
        out_specs=(P(("cent", "dp"), None), P("dp", "cent", None)),
        check_vma=False,
    )
```

profile of v0, /device:TPU:1, one launch (start us, length us, event | category | flops | bytes accessed | tf_op | source)
XLA Modules:
  0.0 496.5 jit_solution(17596930449251836054)
XLA Ops:
  7.2 1.4 copy-done
  8.6 5.1 %multiply_reduce_fusion.1 = (f32[512]{0:T(512)S(1)}, f32[512,1024]{1,0:T(8,128)}) fusion(bf16[512,1536]{1,0:T(8,128)(2,1)S(1)} %copy-done, bf16[1024,1536]{1,0:T(8,128)(2,1)} %param.4), kind=kOutput, calls=%fused_computation.8 | convolution fusion | flops 1611660800 | bytes 6817792 | tf_op jit(solution)/shard_map/id,kd->ik/dot_general | solution.py:28
  13.6 28.6 %pmax.14 = f32[512]{0:T(512)S(1)} all-reduce(f32[512]{0:T(512)S(1)} %get-tuple-element.2), channel_id=1, replica_groups=mesh['cent'=16,'dp'=8] {'cent'}, use_global_device_ids=true, to_apply=%region_1.0 | all-reduce | flops 512 | bytes 4096 | tf_op jit(solution)/shard_map/pmax | solution.py:11
  42.3 2.1 fusion.5
  44.3 30.3 %psum.28 = f32[512]{0:T(512)S(1)} all-reduce(f32[512]{0:T(512)S(1)} %fusion.5), channel_id=1, replica_groups=mesh['cent'=16,'dp'=8] {'cent'}, use_global_device_ids=true, to_apply=%region_3.0 | all-reduce | flops 512 | bytes 4096 | tf_op jit(solution)/shard_map/psum | solution.py:13
  74.7 6.3 %fusion.6 = f32[1024,1536]{1,0:T(8,128)} fusion(bf16[512,1536]{1,0:T(8,128)(2,1)S(1)} %copy-done, f32[512,1024]{1,0:T(8,128)} %get-tuple-element.3, f32[512]{0:T(512)S(1)} %psum.28, f32[512]{0:T(512)S(1)} %pmax.14), kind=kOutput, calls=%fused_computation.11 | convolution fusion | flops 1612709888 | bytes 9965568 | tf_op jit(solution)/shard_map/ik,id->kd/dot_general | solution.py:30
  80.9 0.0 reduce-scatter.2.cloned.1.call-start
  81.0 2.1 fusion.12
  83.1 28.6 %psum.30 = f32[1024]{0:T(1024)S(1)} all-reduce(f32[1024]{0:T(1024)S(1)} %fusion.12), channel_id=1, replica_groups=mesh['cent'=16,'dp'=8] {'dp'}, use_global_device_ids=true, to_apply=%region_6.0 | all-reduce | flops 1024 | bytes 8192 | tf_op jit(solution)/shard_map/psum | solution.py:36
  111.7 232.5 %all-reduce.3.cloned.1.call-done = f32[1024,1536]{1,0:T(8,128)} async-done(((f32[1024,1536]{1,0:T(8,128)}), f32[1024,1536]{1,0:T(8,128)}) %all-reduce.3.cloned.1.call-update) | async-done | bytes 6291472 | tf_op jit(solution)/shard_map/psum | solution.py:36
  344.3 5.2 %divide_convert_fusion = bf16[1024,1536]{1,0:T(8,128)(2,1)S(1)} fusion(f32[1024,1536]{1,0:T(8,128)} %all-reduce.3.cloned.1.call-done, bf16[1024,1536]{1,0:T(8,128)(2,1)} %param.4, f32[1024]{0:T(1024)S(1)} %broadcast_add_fusion), kind=kLoop, calls=%fused_computation | loop fusion | flops 7864320 | bytes 12587008 | tf_op jit(solution)/shard_map/convert_element_type | solution.py:37
  349.5 5.1 %multiply_reduce_fusion = (f32[1024]{0:T(1024)S(1)}, f32[1024,1024]{0,1:T(8,128)}) fusion(bf16[1024,1536]{1,0:T(8,128)(2,1)S(1)} %divide_convert_fusion, bf16[1024,1536]{1,0:T(8,128)(2,1)S(1)} %copy-done.2), kind=kOutput, calls=%fused_computation.2 | convolution fusion | flops 3223321600 | bytes 10489856 | tf_op jit(solution)/shard_map/kd,jd->kj/dot_general | solution.py:41
  354.6 20.9 %pmax.15 = f32[1024]{0:T(1024)S(1)} all-reduce(f32[1024]{0:T(1024)S(1)} %get-tuple-element.4), channel_id=1, replica_groups=mesh['cent'=16,'dp'=8] {'dp'}, use_global_device_ids=true, to_apply=%region_8.0 | all-reduce | flops 1024 | bytes 8192 | tf_op jit(solution)/shard_map/pmax | solution.py:19
  375.5 2.9 fusion.1
  378.4 17.9 %psum.31 = f32[1024]{0:T(1024)S(1)} all-reduce(f32[1024]{0:T(1024)S(1)} %fusion.1), channel_id=1, replica_groups=mesh['cent'=16,'dp'=8] {'dp'}, use_global_device_ids=true, to_apply=%region_10.0 | all-reduce | flops 1024 | bytes 8192 | tf_op jit(solution)/shard_map/psum | solution.py:21
  396.3 9.2 %fusion.2 = f32[1024,1536]{1,0:T(8,128)} fusion(bf16[1024,1536]{1,0:T(8,128)(2,1)} %copy-done.1, f32[1024,1024]{0,1:T(8,128)} %get-tuple-element.5, f32[1024]{0:T(1024)S(1)} %psum.31, f32[1024]{0:T(1024)S(1)} %pmax.15), kind=kOutput, calls=%fused_computation.5 | convolution fusion | flops 3225419776 | bytes 13639680 | tf_op jit(solution)/shard_map/kj,kd->jd/dot_general | solution.py:43
  405.6 0.6 copy-done.3
  406.2 0.6 dynamic-slice
  407.5 3.1 fusion.8
  410.5 35.0 %all-reduce = f32[1024]{0:T(1024)S(1)} all-reduce(f32[1024]{0:T(1024)S(1)} %fusion.8), channel_id=3, replica_groups=mesh['cent'=16,'dp'=8] {'cent'}, use_global_device_ids=true, to_apply=%region_13.0.clone | all-reduce | flops 1024 | bytes 8192
  445.6 0.1 dynamic-slice_add_fusion
  445.6 1.8 constant_dynamic-slice_fusion
  447.4 40.4 %reduce-scatter.2.cloned.1.call-done = f32[64,1536]{1,0:T(8,128)} async-done(((f32[1024,1536]{1,0:T(8,128)}), f32[64,1536]{1,0:T(8,128)}) %reduce-scatter.2.cloned.1.call-update) | async-done | bytes 393232 | tf_op jit(solution)/shard_map/reduce_scatter | solution.py:48
  487.8 1.8 fusion.10
  (10 shorter events, 0.1 us)
Async XLA Ops:
  7.2 1.4 copy-start
  7.2 337.1 %all-reduce.3.cloned.1.call-start = ((), (), s32[]{:S(2)}) async-start(), calls=%async_computation.1 | async-start | bytes 12582912 | tf_op jit(solution)/shard_map/psum | solution.py:36
  80.9 406.9 %reduce-scatter.2.cloned.1.call-start = ((), (), s32[]{:S(2)}) async-start(), calls=%async_computation.2 | async-start | bytes 6684672 | tf_op jit(solution)/shard_map/reduce_scatter | solution.py:48
  344.3 5.2 %copy-start.2 = (bf16[1024,1536]{1,0:T(8,128)(2,1)S(1)}, bf16[1024,1536]{1,0:T(8,128)(2,1)}, u32[]{:S(2)}) copy-start(bf16[1024,1536]{1,0:T(8,128)(2,1)} %param.5) | copy-start | bytes 9437188
  349.5 5.1 %copy-start.1 = (bf16[1024,1536]{1,0:T(8,128)(2,1)}, bf16[1024,1536]{1,0:T(8,128)(2,1)S(1)}, u32[]{:S(2)}) copy-start(bf16[1024,1536]{1,0:T(8,128)(2,1)S(1)} %divide_convert_fusion) | copy-start | bytes 9437188
  405.6 0.7 copy-start.3
Sparse Core Ops, SparseCore 0:
  81.1 263.1 all-reduce.2
  405.7 82.0 reduce-scatter.1
where the time goes:
time: 498 us; the launch traced here: 496 us
  waiting for transfers between devices  273 us (55%)
  blocking collectives  161 us (32%)
  matrix products  25.6 us (5%)
  other arithmetic  17.3 us (3%)
  between operations  14.7 us (3%)
    psum x1, waiting for transfers between devices, body(): moved_all, mass_all = lax.psum((moved, mass), 'dp')  233 us
    reduce_scatter x1, waiting for transfers between devices, body(): lax.psum_scatter(moved_two, 'cent', scatter_dimension=0, tiled=True)  40.4 us
    unnamed x1, blocking collectives  35 us
    psum x1, blocking collectives, first_weights(): total = lax.psum(jnp.sum(expo, axis=1), 'cent')  30.3 us
    psum x1, blocking collectives, body(): moved_all, mass_all = lax.psum((moved, mass), 'dp')  28.6 us
    pmax x1, blocking collectives, first_weights(): peak = lax.pmax(local_peak, 'cent')  28.6 us
    pmax x1, blocking collectives, second_weights(): peak = lax.pmax(local_peak, 'dp')  20.9 us
    psum x1, blocking collectives, second_weights(): total = lax.psum(jnp.sum(expo, axis=1), 'dp')  17.9 us
  transfers between devices with their start and end apart: 2, of which 2 were waited for; matrix products, arithmetic and copies ran while one was open for 2% of the time, Pallas kernels for 0%

commit v1 on v0

v1 whole, which is shorter than its diff:
```python
import jax
import jax.numpy as jnp
from jax import lax
from jax.experimental import pallas as pl
from jax.experimental.pallas import tpu as pltpu
from jax.sharding import PartitionSpec as P

prior = 0.1
MESH = pl.DeviceIdType.MESH
f32, bf16 = jnp.float32, jnp.bfloat16
NT = (((1,), (1,)), ((), ()))
NN = (((1,), (0,)), ((), ()))
D = 1536
SHARD = 512
ROWS = 1024
NX = (256, 128)
NQ = ((SHARD - NX[0]) // 4, (SHARD - NX[1]) // 4)
HX = (NX[0] // 2, NX[1] // 2)
HQ = (NQ[0] // 2, NQ[1] // 2)
KAPPA = D ** -0.5 * 1.4426950408889634
ORDER = (1, 3, 2)


def xor4(v, r):
    if r == 0:
        return v
    if r == 1:
        return v + 1 - 2 * lax.rem(v, 2)
    if r == 2:
        return lax.rem(v + 2, 4)
    return 3 - v


def flip(v, r):
    return 1 - v if r else v


def kernel(images, cents, tops, out1, out2,
           img, ce, to, S, Pb, acc, mass, data, stat, stat2, msum, dsend, drecv, snd, rcv,
           gs, gr, ss, sr, s2s, s2r, mss, msr, ds, dr, rs, rr, ld):
    ci = lax.axis_index("cent")
    di = lax.axis_index("dp")
    y, zl, c = lax.div(ci, 4), lax.rem(lax.div(ci, 2), 2), lax.rem(ci, 2)
    x, zh = lax.div(di, 2), lax.rem(di, 2)

    def dev(x, y, zh, zl, c):
        return ((y * 2 + zl) * 2 + c, x * 2 + zh)

    def centpeer(r):
        return dev(x, xor4(y, r // 4), zh, flip(zl, (r // 2) % 2), flip(c, r % 2))

    def dppeer(r):
        return dev(xor4(x, r // 2), y, flip(zh, r % 2), zl, c)

    partner = centpeer(1)
    zpeer = dev(x, y, 1 - zh, 1 - zl, c)

    l_img = pltpu.make_async_copy(images, img.at[0, 0], ld.at[0])
    l_ce = pltpu.make_async_copy(cents, ce, ld.at[1])
    l_img.start()
    l_ce.start()
    l_to = []
    for b in range(16):
        yy, zz, cc = b // 4, (b // 2) % 2, b % 2
        pos = cc * 512 + yy * 128 + zz * 64
        l_to.append(pltpu.make_async_copy(tops.at[pl.ds(b * 64, 64)], to.at[pl.ds(pos, 64)], ld.at[2 + b]))

    barrier = pltpu.get_barrier_semaphore()
    everyone = [centpeer(r) for r in range(1, 16)] + [dppeer(r) for r in range(1, 8)] + [zpeer]
    for p in everyone:
        pl.semaphore_signal(barrier, inc=1, device_id=p, device_id_type=MESH)
    pl.semaphore_wait(barrier, len(everyone))

    names = {}

    def copy(name, src, dst, device):
        i = len(names)
        names[name] = pltpu.make_async_remote_copy(
            src_ref=src, dst_ref=dst, send_sem=gs.at[i], recv_sem=gr.at[i],
            device_id=device, device_id_type=MESH)

    def rx(z, core):
        return pl.ds(pl.multiple_of(core * HX[z], HX[z]), HX[z])

    def rq(z, q, core):
        return pl.ds(pl.multiple_of(NX[z] + q * NQ[z] + core * HQ[z], 16), HQ[z])

    copy("zx", img.at[0, 0, rx(1, c)], img.at[1, 0, rx(1, c)], zpeer)
    for k in range(4):
        rows = rq(1, xor4(y, k), c)
        copy(("zq", k), img.at[0, 0, rows], img.at[1, 0, rows], zpeer)
    for z in range(2):
        for r in ORDER:
            device = dev(xor4(x, r), y, zh, zl, c)
            copy(("xq", z, r), img.at[z, 0, rq(z, y, c)], img.at[z, r, rq(z, y, c)], device)
            copy(("xx", z, r), img.at[z, 0, rx(z, c)], img.at[z, r, rx(z, c)], device)
        for r in ORDER:
            device = dev(x, xor4(y, r), zh, zl, c)
            rows = rq(z, y, c)
            copy(("yq", z, r), img.at[z, pl.ds(1, 3), rows], img.at[z, pl.ds(1, 3), rows], device)
    copy("dzx", img.at[1, 0, rx(1, c)], img.at[1, 0, rx(1, c)], partner)
    for k in range(4):
        rows = rq(1, xor4(y, k), c)
        copy(("dzq", k), img.at[1, 0, rows], img.at[1, 0, rows], partner)
    for z in range(2):
        for r in ORDER:
            copy(("dxx", z, r), img.at[z, r, rx(z, c)], img.at[z, r, rx(z, c)], partner)
        rows = rq(z, y, c)
        copy(("dxq", z), img.at[z, pl.ds(1, 3), rows], img.at[z, pl.ds(1, 3), rows], partner)
        for r in ORDER:
            rows = rq(z, xor4(y, r), c)
            copy(("dyq", z, r), img.at[z, pl.ds(1, 3), rows], img.at[z, pl.ds(1, 3), rows], partner)

    def start(*ns):
        for n in ns:
            names[n].start()

    def arrive(*ns):
        for n in ns:
            names[n].wait_recv()

    def relay(*pairs):
        for n, m in pairs:
            arrive(n)
            start(m)

    l_img.wait()
    start(*[("xq", 0, r) for r in ORDER])
    start("zx", ("zq", 0))
    start(("xx", 0, 1), ("xx", 0, 3))
    start(("zq", 1), ("zq", 3), ("zq", 2))
    start(("xx", 0, 2))
    for l in l_to:
        l.start()
    l_ce.wait()

    mass[...] = jnp.zeros_like(mass)
    acc[...] = jnp.zeros_like(acc)

    def softmax_pass(sl, cols):
        m = jnp.max(S[sl], axis=0, keepdims=True)

        def tile(j, l):
            rows = pl.ds(pl.multiple_of(j * 128, 128), 128)
            e = jnp.exp2((S[sl, rows, :] - m) * KAPPA)
            S[sl, rows, :] = e
            return l + jnp.sum(e.reshape(16, 8, cols), axis=0)

        l = lax.fori_loop(0, ROWS // 128, tile, jnp.zeros((8, cols), f32))
        return m, jnp.sum(l, axis=0, keepdims=True)

    def stat_copies(buf, j, count, ssem, rsem, peer):
        return [pltpu.make_async_remote_copy(
            src_ref=buf.at[j, 0], dst_ref=buf.at[j, r], send_sem=ssem.at[j], recv_sem=rsem.at[j],
            device_id=peer(r), device_id_type=MESH) for r in range(1, count)]

    def scores_chunk(j, z, xr):
        sl = j % 2
        for n in range(2):
            cols = slice(n * 256, (n + 1) * 256)
            S[sl, :, cols] = lax.dot_general(ce[...], img[z, xr, cols, :], NT, preferred_element_type=f32)
        m, l = softmax_pass(sl, 512)
        stat[j, 0, 0:1, :] = m
        stat[j, 0, 1:2, :] = l
        for cp in stat_copies(stat, j, 16, ss, sr, centpeer):
            cp.start()

    def combine(buf, j, count):
        ms = [buf[j, r, 0:1, :] for r in range(count)]
        M = ms[0]
        for v in ms[1:]:
            M = jnp.maximum(M, v)
        L = jnp.zeros_like(M)
        for r in range(count):
            L = L + buf[j, r, 1:2, :] * jnp.exp2((ms[r] - M) * KAPPA)
        return jnp.exp2((ms[0] - M) * KAPPA) / L

    def wait_bytes(ref, sem):
        pltpu.make_async_copy(ref, ref, sem).wait()

    def weights(sl, f, c0, cols):
        @pl.loop(0, ROWS // 128)
        def _(t):
            rows = pl.ds(pl.multiple_of(t * 128, 128), 128)
            p = S[sl, rows, :] * f
            Pb[rows, c0:c0 + cols] = p.astype(bf16)
            q = p[:, 0:128]
            for i in range(1, cols // 128):
                q = q + p[:, i * 128:(i + 1) * 128]
            mass[rows, :] += q

    def moved_chunk(j, z, xr):
        sl = j % 2
        wait_bytes(stat.at[j, pl.ds(1, 15)], sr.at[j])
        f = combine(stat, j, 16)
        weights(sl, f, 0, 512)

        @pl.loop(0, 2)
        def _(t):
            rows = pl.ds(pl.multiple_of(t * 512, 512), 512)
            p = Pb[rows, 0:512]
            for d in range(3):
                cols = slice(d * 512, (d + 1) * 512)
                acc[rows, cols] += lax.dot_general(p, img[z, xr, :, cols], NN, preferred_element_type=f32)

    def ygo(z):
        arrive(*[("xq", z, r) for r in ORDER])
        start(*[("yq", z, r) for r in ORDER], ("dxq", z))

    def xgo1():
        relay(("zx", "dzx"), (("zq", 0), ("dzq", 0)))
        start(*[("xq", 1, r) for r in ORDER])
        start(*[("xx", 1, r) for r in ORDER])

    seq = [(0, 0), (0, 1), (0, 3), (1, 0), (0, 2), (1, 1), (1, 3), (1, 2)]

    scores_chunk(0, 0, 0)
    ygo(0)
    xgo1()
    moved_chunk(0, 0, 0)
    relay((("xx", 0, 1), ("dxx", 0, 1)), (("xx", 0, 3), ("dxx", 0, 3)))
    relay(*[(("yq", 0, r), ("dyq", 0, r)) for r in ORDER])
    arrive(("dxx", 0, 1), ("dxq", 0), *[("dyq", 0, r) for r in ORDER])
    scores_chunk(1, 0, 1)
    ygo(1)
    arrive(("dxx", 0, 3))
    scores_after = {}
    for j in range(1, 8):
        z, xr = seq[j]
        if j + 1 < 8:
            nz, nx = seq[j + 1]
            if (nz, nx) == (1, 0):
                relay(*[(("zq", k), ("dzq", k)) for k in (1, 3, 2)])
                arrive("dzx", *[("dzq", k) for k in range(4)])
            if (nz, nx) == (0, 2):
                relay((("xx", 0, 2), ("dxx", 0, 2)))
                arrive(("dxx", 0, 2))
            if (nz, nx) == (1, 1):
                relay(*[(("xx", 1, r), ("dxx", 1, r)) for r in (1, 3)])
                relay(*[(("yq", 1, r), ("dyq", 1, r)) for r in ORDER])
                arrive(("dxx", 1, 1), ("dxx", 1, 3), ("dxq", 1), *[("dyq", 1, r) for r in ORDER])
            if (nz, nx) == (1, 2):
                relay((("xx", 1, 2), ("dxx", 1, 2)))
                arrive(("dxx", 1, 2))
            scores_chunk(j + 1, nz, nx)
        moved_chunk(j, z, xr)

    inv = 1.0 / (jnp.sum(mass[...], axis=1, keepdims=True) + prior)
    data[...] = ((acc[...] + prior * ce[...].astype(f32)) * inv).astype(bf16)
    o1 = pltpu.make_async_copy(data.at[pl.ds(pl.multiple_of(di * 128, 128), 128)], out1, ld.at[0])
    o1.start()

    for l in l_to:
        l.wait()
    mass[...] = jnp.zeros_like(mass)
    for h in range(2):
        rows = slice(h * 512, (h + 1) * 512)
        for n in range(2):
            cols = slice(n * 256, (n + 1) * 256)
            S[h, :, cols] = lax.dot_general(
                to[...], data[h * 512 + n * 256:h * 512 + (n + 1) * 256, :], NT, preferred_element_type=f32)
        m, l = softmax_pass(h, 512)
        stat2[h, 0, 0:1, :] = m
        stat2[h, 0, 1:2, :] = l
        for cp in stat_copies(stat2, h, 8, s2s, s2r, dppeer):
            cp.start()
    for h in range(2):
        wait_bytes(stat2.at[h, pl.ds(1, 7)], s2r.at[h])
        weights(h, combine(stat2, h, 8), h * 512, 512)
    msum[0] = jnp.sum(mass[...].T, axis=0, keepdims=True)
    m_copies = [pltpu.make_async_remote_copy(
        src_ref=msum.at[0], dst_ref=msum.at[r], send_sem=mss, recv_sem=msr,
        device_id=centpeer(r), device_id_type=MESH) for r in range(1, 16)]
    for cp in m_copies:
        cp.start()

    def moved_two(base, put):
        @pl.loop(0, 2)
        def _(t):
            src = pl.ds(pl.multiple_of(base + t * 256, 256), 256)
            dst = pl.ds(pl.multiple_of(t * 256, 256), 256)
            p = Pb[src, :]
            for d in range(3):
                cols = slice(d * 512, (d + 1) * 512)
                put(dst, cols, lax.dot_general(p, data[:, cols], NN, preferred_element_type=f32))

    def put_send(rows, cols, v):
        dsend[rows, cols] = v.astype(bf16)

    def put_own(rows, cols, v):
        acc[rows, cols] = v

    moved_two((1 - c) * 512, put_send)
    dcopy = pltpu.make_async_remote_copy(
        src_ref=dsend, dst_ref=drecv, send_sem=ds, recv_sem=dr, device_id=partner, device_id_type=MESH)
    dcopy.start()
    moved_two(c * 512, put_own)
    dcopy.wait_recv()
    blocks = []
    for r in (5, 4, 7, 6, 3, 2, 1):
        yy, zz = xor4(y, r // 2), flip(zl, r % 2)
        rows = pl.ds(pl.multiple_of(yy * 128 + zz * 64, 64), 64)
        snd[r] = (acc[rows, :] + drecv[rows, :].astype(f32)).astype(bf16)
        cp = pltpu.make_async_remote_copy(
            src_ref=snd.at[r], dst_ref=rcv.at[r], send_sem=rs.at[r], recv_sem=rr.at[r],
            device_id=dev(x, yy, zh, zz, c), device_id_type=MESH)
        cp.start()
        blocks.append(cp)
    rows = pl.ds(pl.multiple_of(y * 128 + zl * 64, 64), 64)
    trows = pl.ds(pl.multiple_of(c * 512 + y * 128 + zl * 64, 64), 64)
    wait_bytes(msum.at[pl.ds(1, 15)], msr)
    total = msum[0]
    for r in range(1, 16):
        total = total + msum[r]
    here = c * 512 + y * 128 + zl * 64
    lane = lax.broadcasted_iota(jnp.int32, (64, ROWS), 1)
    sub = lax.broadcasted_iota(jnp.int32, (64, ROWS), 0)
    col = jnp.sum(jnp.where(lane == sub + here, total, 0.0), axis=1, keepdims=True)
    own = acc[rows, :] + drecv[rows, :].astype(f32) + prior * to[trows, :].astype(f32)
    for cp in blocks:
        cp.wait_recv()
    for r in range(1, 8):
        own = own + rcv[r].astype(f32)
    snd[0] = (own * (1.0 / (col + prior))).astype(bf16)
    o2 = pltpu.make_async_copy(snd.at[0], out2.at[0], ld.at[1])
    o2.start()

    for cp in names.values():
        cp.wait_send()
    for j in range(8):
        wait_bytes(stat.at[j, pl.ds(1, 15)], ss.at[j])
    for h in range(2):
        wait_bytes(stat2.at[h, pl.ds(1, 7)], s2s.at[h])
    wait_bytes(msum.at[pl.ds(1, 15)], mss)
    dcopy.wait_send()
    for cp in blocks:
        cp.wait_send()
    o1.wait()
    o2.wait()


def body(images, cents, tops):
    anyspec = pl.BlockSpec(memory_space=pl.ANY)
    ncopies = 42
    flops = 2 * 2 * (1024 * 4096 + 1024 * 1024) * D
    return pl.pallas_call(
        kernel,
        out_shape=(jax.ShapeDtypeStruct((128, D), bf16), jax.ShapeDtypeStruct((1, 64, D), bf16)),
        in_specs=[anyspec] * 3,
        out_specs=(anyspec, anyspec),
        scratch_shapes=[
            pltpu.VMEM((2, 4, SHARD, D), bf16),
            pltpu.VMEM((ROWS, D), bf16),
            pltpu.VMEM((ROWS, D), bf16),
            pltpu.VMEM((2, ROWS, 512), f32),
            pltpu.VMEM((ROWS, 1024), bf16),
            pltpu.VMEM((ROWS, D), f32),
            pltpu.VMEM((ROWS, 128), f32),
            pltpu.VMEM((ROWS, D), bf16),
            pltpu.VMEM((8, 16, 2, 512), f32),
            pltpu.VMEM((2, 8, 2, 512), f32),
            pltpu.VMEM((16, 1, 1024), f32),
            pltpu.VMEM((512, D), bf16),
            pltpu.VMEM((512, D), bf16),
            pltpu.VMEM((8, 64, D), bf16),
            pltpu.VMEM((8, 64, D), bf16),
            pltpu.SemaphoreType.DMA((ncopies,)),
            pltpu.SemaphoreType.DMA((ncopies,)),
            pltpu.SemaphoreType.DMA((8,)),
            pltpu.SemaphoreType.DMA((8,)),
            pltpu.SemaphoreType.DMA((2,)),
            pltpu.SemaphoreType.DMA((2,)),
            pltpu.SemaphoreType.DMA,
            pltpu.SemaphoreType.DMA,
            pltpu.SemaphoreType.DMA,
            pltpu.SemaphoreType.DMA,
            pltpu.SemaphoreType.DMA((8,)),
            pltpu.SemaphoreType.DMA((8,)),
            pltpu.SemaphoreType.DMA((18,)),
        ],
        compiler_params=pltpu.CompilerParams(
            collective_id=0, has_side_effects=True, vmem_limit_bytes=60 * 1024 * 1024),
        cost_estimate=pl.CostEstimate(flops=flops, bytes_accessed=9 * 1024 * 1024, transcendentals=6 * 1024 * 1024),
        name="two_levels",
    )(images, cents, tops)


def solution(mesh):
    return jax.shard_map(
        body,
        mesh=mesh,
        in_specs=(P("dp", None), P("cent", None), P("dp", None)),
        out_specs=(P(("cent", "dp"), None), P("dp", "cent", None)),
        check_vma=False,
    )
```

time: 498 us -> 136 us (0.27)
  waiting for transfers between devices: 273 us -> 0 us
  blocking collectives: 161 us -> 0 us
  Pallas kernels: 0 us -> 131 us
  matrix products: 25.6 us -> 0 us
  other arithmetic: 17.3 us -> 0 us
  between operations: 14.7 us -> 0.64 us
    psum x1 -> x0, waiting for transfers between devices: 233 us -> none  [body(): moved_all, mass_all = lax.psum((moved, mass), 'dp')]
    pallas_call x0 -> x1, Pallas kernels: none -> 131 us  [body(): pl.pallas_call(kernel, out_shape=(jax.ShapeDtypeStruct((128, D), bf16), j...]
    psum x3 -> x0, blocking collectives: 76.8 us -> none  [the longest x1 30.3 us: first_weights(): total = lax.psum(jnp.sum(expo, axis=1), 'cent')]
    pmax x2 -> x0, blocking collectives: 49.5 us -> none  [the longest x1 28.6 us: first_weights(): peak = lax.pmax(local_peak, 'cent')]
    reduce_scatter x1 -> x0, waiting for transfers between devices: 40.4 us -> none  [body(): lax.psum_scatter(moved_two, 'cent', scatter_dimension=0, tiled=True)]
    unnamed x1 -> x0, blocking collectives: 35 us -> none
    dot_general x4 -> x0, matrix products: 25.6 us -> none  [the longest x1 9.24 us: body(): jnp.einsum('kj,kd->jd', resp_two.astype(jnp.bfloat16), data, preferred_el...]
    reduce_sum x4 -> x0, other arithmetic: 10.2 us -> none  [the longest x1 3.08 us: body(): mass_two = jnp.sum(resp_two, axis=0)]
  transfers between devices with their start and end apart: 2 -> 0, of which waited for: 2 -> 0; matrix products, arithmetic and copies ran while one was open for 2% -> 0% of each run, Pallas kernels for 0% -> 0%
where the time goes in v1:
time: 136 us
  Pallas kernels  131 us (96%)
  local copies, waits for them, and re-layouts  3.38 us (2%)
    pallas_call x1, Pallas kernels, body(): pl.pallas_call(kernel, out_shape=(jax.ShapeDtypeStruct((128, D), bf16), j...  131 us
    unnamed x2, local copies, waits for them, and re-layouts  3.38 us

profile of v1, /device:TPU:1, one launch (start us, length us, event | category | flops | bytes accessed | tf_op | source)
XLA Modules:
  0.0 135.5 jit_solution(4743778004781211597)
XLA Ops:
  0.6 131.5 %two_levels.1 = (bf16[128,1536]{1,0:T(8,128)(2,1)}, bf16[1,64,1536]{2,1,0:T(8,128)(2,1)}) custom-call(bf16[512,1536]{1,0:T(8,128)(2,1)} %images.1, bf16[1024,1536]{1,0:T(8,128)(2,1)} %cents.1, bf16[1024,1536]{1,0:T(8,128)(2,1)} %tops.1), custom_call_target="tpu_custom_call" | custom-call | flops 32212254720 | bytes 9437184 | tf_op jit(solution)/shard_map/two_levels/pallas_call | solution.py:346
  132.1 1.8 %copy.7 = bf16[128,1536]{1,0:T(8,128)(2,1)} copy(bf16[128,1536]{1,0:T(8,128)(2,1)} %get-tuple-element.4) | data formatting | bytes 786432
  133.9 1.6 %copy.8 = bf16[1,64,1536]{2,1,0:T(8,128)(2,1)} copy(bf16[1,64,1536]{2,1,0:T(8,128)(2,1)} %get-tuple-element.5) | data formatting | bytes 393216

commit v2 on v1

v2 whole, which is shorter than its diff:
```python
import jax
import jax.numpy as jnp
from jax import lax
from jax.experimental import pallas as pl
from jax.experimental.pallas import tpu as pltpu
from jax.sharding import PartitionSpec as P

prior = 0.1
MESH = pl.DeviceIdType.MESH
f32, bf16 = jnp.float32, jnp.bfloat16
NT = (((1,), (1,)), ((), ()))
NN = (((1,), (0,)), ((), ()))
D = 1536
SHARD = 512
ROWS = 1024
HX, HQ = 128, 32
KAPPA = D ** -0.5 * 1.4426950408889634
ORDER = (1, 3, 2)
AT_X = {(0, 1): 1024, (0, 3): 1152, (0, 2): 2048, (1, 1): 2560, (1, 3): 3072, (1, 2): 3584}
AT_Y = {(0, 1): 1536, (0, 3): 1792, (0, 2): 2304, (1, 1): 2816, (1, 3): 3328, (1, 2): 3840}
CHUNKS = (0, 1024, 1536, 512, 2048, 2560, 3072, 3584)
SLOTS = 4
FIRST = (
    ('xx', 1, 0), ('xx', 3, 0), ('xq', 0, 1), ('xq', 0, 3), ('zr', 0), ('zq',), ('zr', 1), ('zr', 2),
    ('zr', 3), ('xx', 1, 1), ('xx', 3, 1), ('xq', 0, 2),
)
SECOND = (
    ('xq', 1, 1), ('xq', 1, 3), ('xq', 1, 2), ('dzq',),
)
STEPS = (
    ('B', 0, 0), ('xr', 1, 0), ('xr', 3, 0), ('zrs', 0), ('B', 0, 1), ('zqs',), ('yf', 0, 1), ('yf', 0, 3),
    ('zrs', 1), ('A', 1, 0), ('zrs', 2), ('zrs', 3), ('yr', 0, 1, 1), ('yr', 0, 1, 3), ('xr', 1, 1),
    ('xr', 3, 1), ('zis', 0), ('zis', 1), ('yr', 0, 3, 1), ('yr', 0, 3, 3), ('zis', 2), ('yf', 0, 2),
    ('yr', 0, 1, 2), ('A', 1, 1), ('zis', 3), ('A', 1, 2), ('yf', 1, 1), ('yr', 0, 3, 2), ('A', 2, 0),
    ('l', 1), ('xr', 2, 0), ('yr', 0, 2, 3), ('yr', 0, 2, 1), ('A', 2, 1), ('A', 2, 2), ('A', 3, 0),
    ('yf', 1, 3), ('A', 3, 1), ('l', 3), ('yr', 0, 2, 2), ('yr', 1, 1, 1), ('yr', 1, 1, 3), ('A', 3, 2),
    ('xr', 2, 1), ('B', 1, 0), ('yf', 1, 2), ('B', 1, 1), ('lis', 1), ('yr', 1, 3, 3), ('yr', 1, 3, 1),
    ('A', 4, 0), ('yr', 1, 1, 2), ('A', 4, 1), ('A', 4, 2), ('A', 5, 0), ('l', 2), ('lis', 3),
    ('yr', 1, 2, 1), ('yr', 1, 2, 3), ('A', 5, 1), ('yr', 1, 3, 2), ('A', 5, 2), ('B', 2, 0), ('B', 2, 1),
    ('yr', 1, 2, 2), ('A', 6, 0), ('A', 6, 1), ('lis', 2), ('A', 6, 2), ('B', 3, 0), ('B', 3, 1), ('A', 7, 0),
    ('A', 7, 1), ('A', 7, 2), ('B', 4, 0), ('B', 4, 1), ('B', 5, 0), ('B', 5, 1), ('B', 6, 0), ('B', 6, 1),
    ('B', 7, 0), ('B', 7, 1),
)


def xor4(v, r):
    if r == 0:
        return v
    if r == 1:
        return v + 1 - 2 * lax.rem(v, 2)
    if r == 2:
        return lax.rem(v + 2, 4)
    return 3 - v


def flip(v, r):
    return 1 - v if r else v


def kernel(images, cents, tops, out1, out2,
           img, ce, to, S, Pb, acc, mass, data, stat, stat2, msum, dsend, drecv, zs, zr, ys, yr, y2s, y2r, z2s, z2r, res,
           gs, gr, ss, sr, s2s, s2r, mss, msr, ds, dr, rs, rr, ld):
    ci = lax.axis_index("cent")
    di = lax.axis_index("dp")
    y, zl, c = lax.div(ci, 4), lax.rem(lax.div(ci, 2), 2), lax.rem(ci, 2)
    x, zh = lax.div(di, 2), lax.rem(di, 2)

    def dev(x, y, zh, zl, c):
        return ((y * 2 + zl) * 2 + c, x * 2 + zh)

    def centpeer(r):
        return dev(x, xor4(y, r // 4), zh, flip(zl, (r // 2) % 2), flip(c, r % 2))

    def dppeer(r):
        return dev(xor4(x, r // 2), y, flip(zh, r % 2), zl, c)

    partner = centpeer(1)
    zpeer = dev(x, y, 1 - zh, 1 - zl, c)

    l_img = pltpu.make_async_copy(images, img.at[pl.ds(0, SHARD)], ld.at[0])
    l_ce = pltpu.make_async_copy(cents, ce, ld.at[1])
    l_img.start()
    l_ce.start()
    l_to = []
    for b in range(16):
        yy, zz, cc = b // 4, (b // 2) % 2, b % 2
        pos = cc * 512 + yy * 128 + zz * 64
        l_to.append(pltpu.make_async_copy(tops.at[pl.ds(b * 64, 64)], to.at[pl.ds(pos, 64)], ld.at[2 + b]))

    barrier = pltpu.get_barrier_semaphore()
    everyone = [centpeer(r) for r in range(1, 16)] + [dppeer(r) for r in range(1, 8)] + [zpeer]
    for p in everyone:
        pl.semaphore_signal(barrier, inc=1, device_id=p, device_id_type=MESH)

    names = {}

    def copy(name, src, dst, device):
        i = len(names)
        names[name] = pltpu.make_async_remote_copy(
            src_ref=src, dst_ref=dst, send_sem=gs.at[i], recv_sem=gr.at[i],
            device_id=device, device_id_type=MESH)

    def rq(at, q, core):
        return pl.ds(pl.multiple_of(at + q * 64 + core * HQ, 16), HQ)

    def rqh(at, q, core, h):
        return pl.ds(pl.multiple_of(at + q * 64 + core * HQ + h * 16, 16), 16)

    def rxh(at, core, h):
        return pl.ds(pl.multiple_of(at + core * HX + h * 64, 16), 64)

    def near(s, core, h):
        if s == 2:
            return rxh(AT_X[0, 2], core, h)
        return pl.ds(pl.multiple_of(AT_X[0, s] + h * 256 + core * 64, 16), 64)

    zinner = centpeer(2)
    rows = rq(256, y, c)
    rows1 = rq(768, y, c)
    copy(("zq",), img.at[rows], img.at[rows1], zpeer)
    copy(("dzq",), img.at[rows1], img.at[rows1], partner)
    for k in range(4):
        def part(at, h):
            return rxh(at, c, h) if k == 0 else rqh(at + 256, xor4(y, k), c, h)
        copy(("zr", k), img.at[part(0, 1 - zl)], img.at[part(512, 1 - zl)], zpeer)
        copy(("zi", k), img.at[part(512, zl)], img.at[part(512, zl)], zinner)
        copy(("dzr", k), img.at[part(512, zl)], img.at[part(512, zl)], partner)
        copy(("dzi", k), img.at[part(512, 1 - zl)], img.at[part(512, 1 - zl)], partner)
    for s in ORDER:
        device = dev(xor4(x, s), y, zh, zl, c)
        for h in range(2):
            if s != 2:
                copy(("xx", s, h), img.at[rxh(0, c, h)], img.at[near(s, c, h)], device)
            copy(("dxx", s, h), img.at[near(s, c, h)], img.at[near(s, c, h)], partner)
        if s != 2:
            h = 0 if s == 1 else 1
            copy(("xf", s), img.at[near(s, c, h)], img.at[near(2, c, h)], dev(xor4(x, 4 - s), y, zh, zl, c))
        b = AT_X[1, s]
        copy(("lr", s), img.at[near(s, c, 1 - zl)], img.at[rxh(b, c, 1 - zl)], zpeer)
        copy(("li", s), img.at[rxh(b, c, zl)], img.at[rxh(b, c, zl)], zinner)
        copy(("dlr", s), img.at[rxh(b, c, zl)], img.at[rxh(b, c, zl)], partner)
        copy(("dli", s), img.at[rxh(b, c, 1 - zl)], img.at[rxh(b, c, 1 - zl)], partner)
        for z in range(2):
            rows = rq(AT_Y[z, s], y, c)
            copy(("xq", z, s), img.at[rq(z * SHARD + 256, y, c)], img.at[rows], device)
            for r in (1, 3):
                copy(("yq", z, s, r), img.at[rows], img.at[rows], dev(x, xor4(y, r), zh, zl, c))
                there = rqh(AT_Y[z, s], xor4(y, r), c, 0 if r == 1 else 1)
                copy(("yh", z, s, r), img.at[there], img.at[there], dev(x, xor4(y, 4 - r), zh, zl, c))
            for r in range(4):
                there = rq(AT_Y[z, s], xor4(y, r), c)
                copy(("dq", z, s, r), img.at[there], img.at[there], partner)

    def start(*ns):
        for n in ns:
            names[n].start()

    here_now = set()

    def arrive(*ns):
        for n in ns:
            if n not in here_now:
                here_now.add(n)
                names[n].wait_recv()

    relay = {("zqs",): ([("zq",)], SECOND)}
    for k in range(4):
        relay["zrs", k] = ([("zr", k)], [("zi", k), ("dzr", k)])
        relay["zis", k] = ([("zi", k)], [("dzi", k)])
    for s in ORDER:
        relay["l", s] = ([("lr", s)], [("li", s), ("dlr", s)])
        relay["lis", s] = ([("li", s)], [("dli", s)])
        if s == 2:
            relay["xr", 2, 0] = ([("xf", 1)], [("dxx", 2, 0)])
            relay["xr", 2, 1] = ([("xf", 1), ("xf", 3)], [("lr", 2), ("dxx", 2, 1)])
        else:
            relay["xr", s, 0] = ([("xx", s, 0)], ([("xf", s)] if s == 1 else []) + [("dxx", s, 0)])
            relay["xr", s, 1] = ([("xx", s, 0), ("xx", s, 1)],
                                 ([("xf", s)] if s == 3 else []) + [("lr", s), ("dxx", s, 1)])
        for z in range(2):
            relay["yf", z, s] = ([("xq", z, s)], [("yq", z, s, 1), ("yq", z, s, 3), ("dq", z, s, 0)])
            for r in (1, 3):
                relay["yr", z, s, r] = ([("yq", z, s, r)], [("yh", z, s, r), ("dq", z, s, r)])
            relay["yr", z, s, 2] = ([("yh", z, s, 1), ("yh", z, s, 3)], [("dq", z, s, 2)])

    def ready(at):
        if at == 512:
            arrive(("dzr", 0), ("dzi", 0))
        if at == 768:
            arrive(("dzq",), *[(n, k) for n in ("dzr", "dzi") for k in range(1, 4)])
        if at in (1024, 1280):
            h = (at - 1024) // 256
            arrive(("dxx", 1, h), ("dxx", 3, h))
        elif at == AT_X[0, 2]:
            arrive(("dxx", 2, 0), ("dxx", 2, 1))
        for (z, s), a in AT_X.items():
            if z and at == a:
                arrive(("dlr", s), ("dli", s))
        for key, a in AT_Y.items():
            if at == a:
                arrive(*[("dq",) + key + (r,) for r in range(4)])

    l_img.wait()
    l_ce.wait()

    mass[...] = jnp.zeros_like(mass)

    def soft(sl):
        ms, ls = [], []
        for n in (slice(0, 256), slice(256, 512)):
            m = jnp.max(S[sl, :, n], axis=0, keepdims=True)
            l = jnp.zeros((8, 256), f32)
            for t in range(0, ROWS, 128):
                e = jnp.exp2((S[sl, t:t + 128, n] - m) * KAPPA)
                S[sl, t:t + 128, n] = e
                l = l + jnp.sum(e.reshape(16, 8, 256), axis=0)
            ms.append(m)
            ls.append(jnp.sum(l, axis=0, keepdims=True))
        return jnp.concatenate(ms, axis=1), jnp.concatenate(ls, axis=1)

    def stat_copies(buf, j, count, ssem, rsem, peer):
        return [pltpu.make_async_remote_copy(
            src_ref=buf.at[j, 0], dst_ref=buf.at[j, r], send_sem=ssem.at[j], recv_sem=rsem.at[j],
            device_id=peer(r), device_id_type=MESH) for r in range(1, count)]

    def scores(sl, left, right, lo):
        for n in range(2):
            cols = slice(n * 256, (n + 1) * 256)
            S[sl, :, cols] = lax.dot_general(
                left[...], right[lo + n * 256:lo + (n + 1) * 256, :], NT, preferred_element_type=f32)
        return soft(sl)

    def combine(buf, j, count):
        ms = [buf[j, r, 0:1, :] for r in range(count)]
        M = ms[0]
        for v in ms[1:]:
            M = jnp.maximum(M, v)
        L = jnp.zeros_like(M)
        for r in range(count):
            L = L + buf[j, r, 1:2, :] * jnp.exp2((ms[r] - M) * KAPPA)
        return jnp.exp2((ms[0] - M) * KAPPA) / L

    def wait_bytes(ref, sem):
        pltpu.make_async_copy(ref, ref, sem).wait()

    def weights(sl, f, rows):
        p = S[sl, rows, :] * f
        q = p[:, 0:128]
        for i in range(1, 4):
            q = q + p[:, i * 128:(i + 1) * 128]
        mass[rows, :] += q
        return p.astype(bf16)

    def A(j, part):
        at, sl = CHUNKS[j] + 256 * part, j % SLOTS
        if part < 2:
            ready(at)
            S[sl, :, part * 256:(part + 1) * 256] = lax.dot_general(
                ce[...], img[at:at + 256, :], NT, preferred_element_type=f32)
        else:
            m, l = soft(sl)
            stat[j, 0, 0:1, :] = m
            stat[j, 0, 1:2, :] = l
            if j:
                send_stats(j)

    def send_stats(j):
        for cp in stat_copies(stat, j, 16, ss, sr, centpeer):
            cp.start()

    factors = {}

    def B(j, part):
        at = CHUNKS[j]
        if part == 0:
            wait_bytes(stat.at[j, pl.ds(1, 15)], sr.at[j])
            factors[j] = combine(stat, j, 16)
        rows = slice(part * 512, (part + 1) * 512)
        p = weights(j % SLOTS, factors[j], rows)
        for d in range(3):
            cols = slice(d * 512, (d + 1) * 512)
            v = lax.dot_general(p, img[at:at + 512, cols], NN, preferred_element_type=f32)
            if j == 0:
                acc[rows, cols] = v
            else:
                acc[rows, cols] += v

    for part in range(3):
        A(0, part)
    pl.semaphore_wait(barrier, len(everyone))
    start(*FIRST)
    send_stats(0)
    for l in l_to:
        l.start()
    for step in STEPS:
        if step[0] == "A":
            A(*step[1:])
        elif step[0] == "B":
            B(*step[1:])
        else:
            arrive(*relay[step][0])
            start(*relay[step][1])

    for t in range(0, ROWS, 256):
        rows = slice(t, t + 256)
        inv = 1.0 / (jnp.sum(mass[rows, :], axis=1, keepdims=True) + prior)
        data[rows, :] = ((acc[rows, :] + prior * ce[rows, :].astype(f32)) * inv).astype(bf16)
    o1 = pltpu.make_async_copy(data.at[pl.ds(pl.multiple_of(di * 128, 128), 128)], out1, ld.at[0])
    o1.start()

    for l in l_to:
        l.wait()
    mass[...] = jnp.zeros_like(mass)
    for h in range(2):
        m, l = scores(h, to, data, h * 512)
        stat2[h, 0, 0:1, :] = m
        stat2[h, 0, 1:2, :] = l
        for cp in stat_copies(stat2, h, 8, s2s, s2r, dppeer):
            cp.start()
    wait_bytes(stat2.at[0, pl.ds(1, 7)], s2r.at[0])
    f = combine(stat2, 0, 8)
    for t in range(0, ROWS, 512):
        rows = slice(t, t + 512)
        p = weights(0, f, rows)
        for d in range(3):
            cols = slice(d * 512, (d + 1) * 512)
            acc[rows, cols] = lax.dot_general(p, data[0:512, cols], NN, preferred_element_type=f32)
    wait_bytes(stat2.at[1, pl.ds(1, 7)], s2r.at[1])
    f = combine(stat2, 1, 8)
    for t in range(0, ROWS, 512):
        rows = slice(t, t + 512)
        Pb[rows, :] = weights(1, f, rows)
    msum[0] = jnp.sum(mass[...].T, axis=0, keepdims=True)
    m_copies = [pltpu.make_async_remote_copy(
        src_ref=msum.at[0], dst_ref=msum.at[r], send_sem=mss, recv_sem=msr,
        device_id=centpeer(r), device_id_type=MESH) for r in range(1, 16)]
    for cp in m_copies:
        cp.start()

    pair = lax.div(y, 2)
    d_copies = []
    for i in range(2):
        half = pl.multiple_of((1 - pair if i == 0 else pair) * 256, 256)
        src = pl.ds(pl.multiple_of((1 - c) * 512 + half, 256), 256)
        for d in range(3):
            cols = slice(d * 512, (d + 1) * 512)
            v = acc[src, cols] + lax.dot_general(Pb[src, :], data[512:1024, cols], NN, preferred_element_type=f32)
            dsend[pl.ds(half, 256), cols] = v.astype(bf16)
        cp = pltpu.make_async_remote_copy(
            src_ref=dsend.at[pl.ds(half, 256)], dst_ref=drecv.at[pl.ds(half, 256)],
            send_sem=ds.at[i], recv_sem=dr.at[i], device_id=partner, device_id_type=MESH)
        cp.start()
        d_copies.append(cp)
    blocks = []

    def send(i, src, dst, device):
        cp = pltpu.make_async_remote_copy(
            src_ref=src, dst_ref=dst, send_sem=rs.at[i], recv_sem=rr.at[i], device_id=device, device_id_type=MESH)
        cp.start()
        blocks.append(cp)
        return cp

    def at(yy, zz):
        return pl.ds(pl.multiple_of(c * 512 + yy * 128 + zz * 64, 64), 64)

    zpartner = dev(x, y, zh, 1 - zl, c)
    LEFT, RIGHT = slice(0, D // 2), slice(D // 2, D)
    along_y, along_z = {}, {}
    for i in range(2):
        half = pl.multiple_of((1 - pair if i == 0 else pair) * 256, 256)
        src = pl.ds(pl.multiple_of(c * 512 + half, 256), 256)
        for d in range(3):
            cols = slice(d * 512, (d + 1) * 512)
            acc[src, cols] += lax.dot_general(Pb[src, :], data[512:1024, cols], NN, preferred_element_type=f32)
        d_copies[i].wait_recv()
        acc[src, :] += drecv[pl.ds(half, 256), :].astype(f32)
        for r in ((2, 3) if i == 0 else (1, 0)):
            yy = xor4(y, r)
            zs[r] = acc[at(yy, 1 - zl), RIGHT].astype(bf16)
            along_z[r] = send(r, zs.at[r], zr.at[r], zpartner)
            if r:
                rows = pl.ds(pl.multiple_of(c * 512 + yy * 128, 128), 128)
                ys[r] = acc[rows, LEFT].astype(bf16)
                along_y[r] = send(4 + r, ys.at[r], yr.at[r], dev(x, yy, zh, zl, c))
    along_y2 = {}
    for r in (2, 3, 1):
        yy = xor4(y, r)
        along_z[r].wait_recv()
        y2s[r] = (acc[at(yy, zl), RIGHT] + zr[r].astype(f32)).astype(bf16)
        along_y2[r] = send(8 + r, y2s.at[r], y2r.at[r], dev(x, yy, zh, zl, c))
    here = c * 512 + y * 128 + zl * 64
    wait_bytes(msum.at[pl.ds(1, 15)], msr)
    total = msum[0]
    for r in range(1, 16):
        total = total + msum[r]
    lane = lax.broadcasted_iota(jnp.int32, (64, ROWS), 1)
    sub = lax.broadcasted_iota(jnp.int32, (64, ROWS), 0)
    col = jnp.sum(jnp.where(lane == sub + here, total, 0.0), axis=1, keepdims=True)
    inv = 1.0 / (col + prior)
    for r in (2, 3, 1):
        along_y[r].wait_recv()

    def left(zz):
        rows = pl.ds(pl.multiple_of(zz * 64, 64), 64)
        v = acc[at(y, zz), LEFT]
        for r in (1, 2, 3):
            v = v + yr[r, rows, :].astype(f32)
        return v

    z2s[...] = left(1 - zl).astype(bf16)
    along_z2 = send(12, z2s, z2r, zpartner)
    own = left(zl) + prior * to[at(y, zl), LEFT].astype(f32)
    along_z[0].wait_recv()
    right = acc[at(y, zl), RIGHT] + prior * to[at(y, zl), RIGHT].astype(f32) + zr[0].astype(f32)
    for r in (2, 3, 1):
        along_y2[r].wait_recv()
        right = right + y2r[r].astype(f32)
    res[:, RIGHT] = (right * inv).astype(bf16)
    along_z2.wait_recv()
    res[:, LEFT] = ((own + z2r[...].astype(f32)) * inv).astype(bf16)
    o2 = pltpu.make_async_copy(res, out2, ld.at[1])
    o2.start()

    for cp in names.values():
        cp.wait_send()
    for j in range(8):
        wait_bytes(stat.at[j, pl.ds(1, 15)], ss.at[j])
    for h in range(2):
        wait_bytes(stat2.at[h, pl.ds(1, 7)], s2s.at[h])
    wait_bytes(msum.at[pl.ds(1, 15)], mss)
    for cp in d_copies + blocks:
        cp.wait_send()
    o1.wait()
    o2.wait()


def hand_over(a, b, out1, out2):
    out1[...] = a[...]
    out2[0] = b[...]


def body(images, cents, tops):
    anyspec = pl.BlockSpec(memory_space=pl.ANY)
    vmem = pl.BlockSpec(memory_space=pltpu.VMEM)
    ncopies = 96
    flops = 2 * 2 * (1024 * 4096 + 1024 * 1024) * D
    part, top = pl.pallas_call(
        kernel,
        out_shape=(jax.ShapeDtypeStruct((128, D), bf16), jax.ShapeDtypeStruct((64, D), bf16)),
        in_specs=[anyspec] * 3,
        out_specs=(anyspec, anyspec),
        scratch_shapes=[
            pltpu.VMEM((8 * SHARD, D), bf16),
            pltpu.VMEM((ROWS, D), bf16),
            pltpu.VMEM((ROWS, D), bf16),
            pltpu.VMEM((SLOTS, ROWS, 512), f32),
            pltpu.VMEM((ROWS, 512), bf16),
            pltpu.VMEM((ROWS, D), f32),
            pltpu.VMEM((ROWS, 128), f32),
            pltpu.VMEM((ROWS, D), bf16),
            pltpu.VMEM((8, 16, 2, 512), f32),
            pltpu.VMEM((2, 8, 2, 512), f32),
            pltpu.VMEM((16, 1, 1024), f32),
            pltpu.VMEM((512, D), bf16),
            pltpu.VMEM((512, D), bf16),
            pltpu.VMEM((4, 64, D // 2), bf16),
            pltpu.VMEM((4, 64, D // 2), bf16),
            pltpu.VMEM((4, 128, D // 2), bf16),
            pltpu.VMEM((4, 128, D // 2), bf16),
            pltpu.VMEM((4, 64, D // 2), bf16),
            pltpu.VMEM((4, 64, D // 2), bf16),
            pltpu.VMEM((64, D // 2), bf16),
            pltpu.VMEM((64, D // 2), bf16),
            pltpu.VMEM((64, D), bf16),
            pltpu.SemaphoreType.DMA((ncopies,)),
            pltpu.SemaphoreType.DMA((ncopies,)),
            pltpu.SemaphoreType.DMA((8,)),
            pltpu.SemaphoreType.DMA((8,)),
            pltpu.SemaphoreType.DMA((2,)),
            pltpu.SemaphoreType.DMA((2,)),
            pltpu.SemaphoreType.DMA,
            pltpu.SemaphoreType.DMA,
            pltpu.SemaphoreType.DMA((2,)),
            pltpu.SemaphoreType.DMA((2,)),
            pltpu.SemaphoreType.DMA((13,)),
            pltpu.SemaphoreType.DMA((13,)),
            pltpu.SemaphoreType.DMA((18,)),
        ],
        compiler_params=pltpu.CompilerParams(
            collective_id=0, has_side_effects=True, vmem_limit_bytes=60 * 1024 * 1024),
        cost_estimate=pl.CostEstimate(flops=flops, bytes_accessed=9 * 1024 * 1024, transcendentals=6 * 1024 * 1024),
        name="two_levels",
    )(images, cents, tops)
    return pl.pallas_call(
        hand_over,
        out_shape=(jax.ShapeDtypeStruct((128, D), bf16), jax.ShapeDtypeStruct((1, 64, D), bf16)),
        in_specs=[vmem] * 2,
        out_specs=(vmem, vmem),
        name="hand_over",
    )(part, top)


def solution(mesh):
    return jax.shard_map(
        body,
        mesh=mesh,
        in_specs=(P("dp", None), P("cent", None), P("dp", None)),
        out_specs=(P(("cent", "dp"), None), P("dp", "cent", None)),
        check_vma=False,
    )
```

time: 136 us -> 101 us (0.74)
  Pallas kernels: 131 us -> 100 us
  local copies, waits for them, and re-layouts: 3.38 us -> 0 us
    pallas_call x1, Pallas kernels: 131 us -> 98.2 us  [body(): pl.pallas_call(kernel, out_shape=(jax.ShapeDtypeStruct((128, D), bf16), j...]
    unnamed x2 -> x0, local copies, waits for them, and re-layouts: 3.38 us -> none
    pallas_call x0 -> x1, Pallas kernels: none -> 1.88 us  [body(): pl.pallas_call(hand_over, out_shape=(jax.ShapeDtypeStruct((128, D), bf16)...]
where the time goes in v2:
time: 101 us
  Pallas kernels  100 us (99%)
    pallas_call x1, Pallas kernels, body(): pl.pallas_call(kernel, out_shape=(jax.ShapeDtypeStruct((128, D), bf16), j...  98.2 us

profile of v2, /device:TPU:1, one launch (start us, length us, event | category | flops | bytes accessed | tf_op | source)
XLA Modules:
  0.0 100.7 jit_solution(61163843943053671)
XLA Ops:
  0.6 98.2 %two_levels.1 = (bf16[128,1536]{1,0:T(8,128)(2,1)}, bf16[64,1536]{1,0:T(8,128)(2,1)}) custom-call(bf16[512,1536]{1,0:T(8,128)(2,1)} %images.1, bf16[1024,1536]{1,0:T(8,128)(2,1)} %cents.1, bf16[1024,1536]{1,0:T(8,128)(2,1)} %tops.1), custom_call_target="tpu_custom_call" | custom-call | flops 32212254720 | bytes 9437184 | tf_op jit(solution)/shard_map/two_levels/pallas_call | solution.py:447
  98.8 1.9 %hand_over.1 = (bf16[128,1536]{1,0:T(8,128)(2,1)}, bf16[1,64,1536]{2,1,0:T(8,128)(2,1)}) custom-call(bf16[128,1536]{1,0:T(8,128)(2,1)} %get-tuple-element.4.a, bf16[64,1536]{1,0:T(8,128)(2,1)} %get-tuple-element.5.b), custom_call_target="tpu_custom_call" | custom-call | tf_op jit(solution)/shard_map/hand_over/pallas_call | solution.py:494

commit v3 on v2

--- a/solution.py
+++ b/solution.py
@@ -18,7 +18,7 @@
 ORDER = (1, 3, 2)
 AT_X = {(0, 1): 1024, (0, 3): 1152, (0, 2): 2048, (1, 1): 2560, (1, 3): 3072, (1, 2): 3584}
 AT_Y = {(0, 1): 1536, (0, 3): 1792, (0, 2): 2304, (1, 1): 2816, (1, 3): 3328, (1, 2): 3840}
-CHUNKS = (0, 1024, 1536, 512, 2048, 2560, 3072, 3584)
+CHUNKS = (0, 1024, 512, 1536, 2048, 2560, 3072, 3584)
 SLOTS = 4
 FIRST = (
     ('xx', 1, 0), ('xx', 3, 0), ('xq', 0, 1), ('xq', 0, 3), ('zr', 0), ('zq',), ('zr', 1), ('zr', 2),
@@ -28,18 +28,15 @@
     ('xq', 1, 1), ('xq', 1, 3), ('xq', 1, 2), ('dzq',),
 )
 STEPS = (
-    ('B', 0, 0), ('xr', 1, 0), ('xr', 3, 0), ('zrs', 0), ('B', 0, 1), ('zqs',), ('yf', 0, 1), ('yf', 0, 3),
-    ('zrs', 1), ('A', 1, 0), ('zrs', 2), ('zrs', 3), ('yr', 0, 1, 1), ('yr', 0, 1, 3), ('xr', 1, 1),
-    ('xr', 3, 1), ('zis', 0), ('zis', 1), ('yr', 0, 3, 1), ('yr', 0, 3, 3), ('zis', 2), ('yf', 0, 2),
-    ('yr', 0, 1, 2), ('A', 1, 1), ('zis', 3), ('A', 1, 2), ('yf', 1, 1), ('yr', 0, 3, 2), ('A', 2, 0),
-    ('l', 1), ('xr', 2, 0), ('yr', 0, 2, 3), ('yr', 0, 2, 1), ('A', 2, 1), ('A', 2, 2), ('A', 3, 0),
-    ('yf', 1, 3), ('A', 3, 1), ('l', 3), ('yr', 0, 2, 2), ('yr', 1, 1, 1), ('yr', 1, 1, 3), ('A', 3, 2),
-    ('xr', 2, 1), ('B', 1, 0), ('yf', 1, 2), ('B', 1, 1), ('lis', 1), ('yr', 1, 3, 3), ('yr', 1, 3, 1),
-    ('A', 4, 0), ('yr', 1, 1, 2), ('A', 4, 1), ('A', 4, 2), ('A', 5, 0), ('l', 2), ('lis', 3),
-    ('yr', 1, 2, 1), ('yr', 1, 2, 3), ('A', 5, 1), ('yr', 1, 3, 2), ('A', 5, 2), ('B', 2, 0), ('B', 2, 1),
-    ('yr', 1, 2, 2), ('A', 6, 0), ('A', 6, 1), ('lis', 2), ('A', 6, 2), ('B', 3, 0), ('B', 3, 1), ('A', 7, 0),
-    ('A', 7, 1), ('A', 7, 2), ('B', 4, 0), ('B', 4, 1), ('B', 5, 0), ('B', 5, 1), ('B', 6, 0), ('B', 6, 1),
-    ('B', 7, 0), ('B', 7, 1),
+    ('B', 0), ('xr', 1, 0), ('xr', 3, 0), ('zrs', 0), ('zqs',), ('yf', 0, 1), ('yf', 0, 3), ('zrs', 1),
+    ('zrs', 2), ('zrs', 3), ('yr', 0, 1, 1), ('yr', 0, 1, 3), ('xr', 1, 1), ('xr', 3, 1), ('zis', 0),
+    ('yr', 0, 3, 1), ('yr', 0, 3, 3), ('zis', 1), ('yf', 0, 2), ('yr', 0, 1, 2), ('A', 1), ('yf', 1, 1),
+    ('l', 1, 0), ('zis', 2), ('zis', 3), ('yr', 0, 3, 2), ('l', 1, 1), ('xr', 2, 0), ('yr', 0, 2, 3),
+    ('yr', 0, 2, 1), ('A', 2), ('yf', 1, 3), ('l', 3, 0), ('l', 3, 1), ('lis', 1, 0), ('yr', 1, 1, 1),
+    ('yr', 1, 1, 3), ('A', 3), ('yf', 1, 2), ('xr', 2, 1), ('lis', 1, 1), ('yr', 0, 2, 2), ('B', 1),
+    ('lis', 3, 0), ('yr', 1, 3, 1), ('yr', 1, 3, 3), ('A', 4), ('l', 2, 0), ('lis', 3, 1), ('yr', 1, 1, 2),
+    ('B', 2), ('l', 2, 1), ('yr', 1, 3, 2), ('yr', 1, 2, 1), ('yr', 1, 2, 3), ('B', 3), ('lis', 2, 0),
+    ('A', 5), ('lis', 2, 1), ('yr', 1, 2, 2), ('A', 6), ('A', 7), ('B', 4), ('B', 5), ('B', 6), ('B', 7),
 )
 
 
@@ -58,7 +55,7 @@
 
 
 def kernel(images, cents, tops, out1, out2,
-           img, ce, to, S, Pb, acc, mass, data, stat, stat2, msum, dsend, drecv, zs, zr, ys, yr, y2s, y2r, z2s, z2r, res,
+           img, ce, to, S, Pb, acc, mass, data, stat, stat2, msum, dsend, drecv, zs, zr, fs, fr, ys, yr, y2s, y2r, z2s, z2r, res,
            gs, gr, ss, sr, s2s, s2r, mss, msr, ds, dr, rs, rr, ld):
     ci = lax.axis_index("cent")
     di = lax.axis_index("dp")
@@ -109,10 +106,13 @@
     def rxh(at, core, h):
         return pl.ds(pl.multiple_of(at + core * HX + h * 64, 16), 64)
 
+    def near_at(s, core, h):
+        if s == 2:
+            return AT_X[0, 2] + core * HX + h * 64
+        return AT_X[0, s] + h * 256 + core * 64
+
     def near(s, core, h):
-        if s == 2:
-            return rxh(AT_X[0, 2], core, h)
-        return pl.ds(pl.multiple_of(AT_X[0, s] + h * 256 + core * 64, 16), 64)
+        return pl.ds(pl.multiple_of(near_at(s, core, h), 16), 64)
 
     zinner = centpeer(2)
     rows = rq(256, y, c)
@@ -135,11 +135,14 @@
         if s != 2:
             h = 0 if s == 1 else 1
             copy(("xf", s), img.at[near(s, c, h)], img.at[near(2, c, h)], dev(xor4(x, 4 - s), y, zh, zl, c))
-        b = AT_X[1, s]
-        copy(("lr", s), img.at[near(s, c, 1 - zl)], img.at[rxh(b, c, 1 - zl)], zpeer)
-        copy(("li", s), img.at[rxh(b, c, zl)], img.at[rxh(b, c, zl)], zinner)
-        copy(("dlr", s), img.at[rxh(b, c, zl)], img.at[rxh(b, c, zl)], partner)
-        copy(("dli", s), img.at[rxh(b, c, 1 - zl)], img.at[rxh(b, c, 1 - zl)], partner)
+        for g in range(2):
+            def there(core, h):
+                return pl.ds(pl.multiple_of(AT_X[1, s] + core * HX + h * 64 + g * 32, 16), 32)
+            src = pl.ds(pl.multiple_of(near_at(s, c, 1 - zl) + g * 32, 16), 32)
+            copy(("lr", s, g), img.at[src], img.at[there(c, 1 - zl)], zpeer)
+            copy(("li", s, g), img.at[there(c, zl)], img.at[there(c, zl)], zinner)
+            copy(("dlr", s, g), img.at[there(c, zl)], img.at[there(c, zl)], partner)
+            copy(("dli", s, g), img.at[there(c, 1 - zl)], img.at[there(c, 1 - zl)], partner)
         for z in range(2):
             rows = rq(AT_Y[z, s], y, c)
             copy(("xq", z, s), img.at[rq(z * SHARD + 256, y, c)], img.at[rows], device)
@@ -168,15 +171,16 @@
         relay["zrs", k] = ([("zr", k)], [("zi", k), ("dzr", k)])
         relay["zis", k] = ([("zi", k)], [("dzi", k)])
     for s in ORDER:
-        relay["l", s] = ([("lr", s)], [("li", s), ("dlr", s)])
-        relay["lis", s] = ([("li", s)], [("dli", s)])
+        for g in range(2):
+            relay["l", s, g] = ([("lr", s, g)], [("li", s, g), ("dlr", s, g)])
+            relay["lis", s, g] = ([("li", s, g)], [("dli", s, g)])
         if s == 2:
             relay["xr", 2, 0] = ([("xf", 1)], [("dxx", 2, 0)])
-            relay["xr", 2, 1] = ([("xf", 1), ("xf", 3)], [("lr", 2), ("dxx", 2, 1)])
+            relay["xr", 2, 1] = ([("xf", 1), ("xf", 3)], [("lr", 2, 0), ("lr", 2, 1), ("dxx", 2, 1)])
         else:
             relay["xr", s, 0] = ([("xx", s, 0)], ([("xf", s)] if s == 1 else []) + [("dxx", s, 0)])
             relay["xr", s, 1] = ([("xx", s, 0), ("xx", s, 1)],
-                                 ([("xf", s)] if s == 3 else []) + [("lr", s), ("dxx", s, 1)])
+                                 ([("xf", s)] if s == 3 else []) + [("lr", s, 0), ("lr", s, 1), ("dxx", s, 1)])
         for z in range(2):
             relay["yf", z, s] = ([("xq", z, s)], [("yq", z, s, 1), ("yq", z, s, 3), ("dq", z, s, 0)])
             for r in (1, 3):
@@ -195,7 +199,7 @@
             arrive(("dxx", 2, 0), ("dxx", 2, 1))
         for (z, s), a in AT_X.items():
             if z and at == a:
-                arrive(("dlr", s), ("dli", s))
+                arrive(*[(n, s, g) for n in ("dlr", "dli") for g in range(2)])
         for key, a in AT_Y.items():
             if at == a:
                 arrive(*[("dq",) + key + (r,) for r in range(4)])
@@ -251,42 +255,36 @@
         mass[rows, :] += q
         return p.astype(bf16)
 
-    def A(j, part):
-        at, sl = CHUNKS[j] + 256 * part, j % SLOTS
-        if part < 2:
-            ready(at)
-            S[sl, :, part * 256:(part + 1) * 256] = lax.dot_general(
-                ce[...], img[at:at + 256, :], NT, preferred_element_type=f32)
-        else:
-            m, l = soft(sl)
-            stat[j, 0, 0:1, :] = m
-            stat[j, 0, 1:2, :] = l
-            if j:
-                send_stats(j)
+    def A(j):
+        at, sl = CHUNKS[j], j % SLOTS
+        ready(at)
+        ready(at + 256)
+        m, l = scores(sl, ce, img, at)
+        stat[j, 0, 0:1, :] = m
+        stat[j, 0, 1:2, :] = l
+        if j:
+            send_stats(j)
 
     def send_stats(j):
         for cp in stat_copies(stat, j, 16, ss, sr, centpeer):
             cp.start()
 
-    factors = {}
-
-    def B(j, part):
+    def B(j):
         at = CHUNKS[j]
-        if part == 0:
-            wait_bytes(stat.at[j, pl.ds(1, 15)], sr.at[j])
-            factors[j] = combine(stat, j, 16)
-        rows = slice(part * 512, (part + 1) * 512)
-        p = weights(j % SLOTS, factors[j], rows)
-        for d in range(3):
-            cols = slice(d * 512, (d + 1) * 512)
-            v = lax.dot_general(p, img[at:at + 512, cols], NN, preferred_element_type=f32)
-            if j == 0:
-                acc[rows, cols] = v
-            else:
-                acc[rows, cols] += v
-
-    for part in range(3):
-        A(0, part)
+        wait_bytes(stat.at[j, pl.ds(1, 15)], sr.at[j])
+        f = combine(stat, j, 16)
+        for t in range(0, ROWS, 512):
+            rows = slice(t, t + 512)
+            p = weights(j % SLOTS, f, rows)
+            for d in range(3):
+                cols = slice(d * 512, (d + 1) * 512)
+                v = lax.dot_general(p, img[at:at + 512, cols], NN, preferred_element_type=f32)
+                if j == 0:
+                    acc[rows, cols] = v
+                else:
+                    acc[rows, cols] += v
+
+    A(0)
     pl.semaphore_wait(barrier, len(everyone))
     start(*FIRST)
     send_stats(0)
@@ -294,9 +292,9 @@
         l.start()
     for step in STEPS:
         if step[0] == "A":
-            A(*step[1:])
+            A(step[1])
         elif step[0] == "B":
-            B(*step[1:])
+            B(step[1])
         else:
             arrive(*relay[step][0])
             start(*relay[step][1])
@@ -330,13 +328,6 @@
     for t in range(0, ROWS, 512):
         rows = slice(t, t + 512)
         Pb[rows, :] = weights(1, f, rows)
-    msum[0] = jnp.sum(mass[...].T, axis=0, keepdims=True)
-    m_copies = [pltpu.make_async_remote_copy(
-        src_ref=msum.at[0], dst_ref=msum.at[r], send_sem=mss, recv_sem=msr,
-        device_id=centpeer(r), device_id_type=MESH) for r in range(1, 16)]
-    for cp in m_copies:
-        cp.start()
-
     pair = lax.div(y, 2)
     d_copies = []
     for i in range(2):
@@ -351,6 +342,13 @@
             send_sem=ds.at[i], recv_sem=dr.at[i], device_id=partner, device_id_type=MESH)
         cp.start()
         d_copies.append(cp)
+    msum[0] = jnp.sum(mass[...].T, axis=0, keepdims=True)
+    m_copies = [pltpu.make_async_remote_copy(
+        src_ref=msum.at[0], dst_ref=msum.at[r], send_sem=mss, recv_sem=msr,
+        device_id=centpeer(r), device_id_type=MESH) for r in range(1, 16)]
+    for cp in m_copies:
+        cp.start()
+
     blocks = []
 
     def send(i, src, dst, device):
@@ -365,7 +363,7 @@
 
     zpartner = dev(x, y, zh, 1 - zl, c)
     LEFT, RIGHT = slice(0, D // 2), slice(D // 2, D)
-    along_y, along_z = {}, {}
+    first, along_y, along_z = {}, {}, {}
     for i in range(2):
         half = pl.multiple_of((1 - pair if i == 0 else pair) * 256, 256)
         src = pl.ds(pl.multiple_of(c * 512 + half, 256), 256)
@@ -378,10 +376,20 @@
             yy = xor4(y, r)
             zs[r] = acc[at(yy, 1 - zl), RIGHT].astype(bf16)
             along_z[r] = send(r, zs.at[r], zr.at[r], zpartner)
-            if r:
-                rows = pl.ds(pl.multiple_of(c * 512 + yy * 128, 128), 128)
-                ys[r] = acc[rows, LEFT].astype(bf16)
-                along_y[r] = send(4 + r, ys.at[r], yr.at[r], dev(x, yy, zh, zl, c))
+            if r == 2:
+                for h in range(2):
+                    fs[h] = acc[at(yy, h), LEFT].astype(bf16)
+                    first[h] = send(4 + 2 * h, fs.at[h], fr.at[h], dev(x, xor4(y, 1 + 2 * h), zh, zl, c))
+    for r in (3, 1):
+        yy = xor4(y, r)
+        h = 0 if r == 3 else 1
+        first[h].wait_recv()
+        for zz in range(2):
+            v = acc[at(yy, zz), LEFT]
+            if zz == h:
+                v = v + fr[h].astype(f32)
+            ys[r, zz * 64:(zz + 1) * 64, :] = v.astype(bf16)
+        along_y[r] = send(4 + r, ys.at[r], yr.at[r], dev(x, yy, zh, zl, c))
     along_y2 = {}
     for r in (2, 3, 1):
         yy = xor4(y, r)
@@ -397,13 +405,13 @@
     sub = lax.broadcasted_iota(jnp.int32, (64, ROWS), 0)
     col = jnp.sum(jnp.where(lane == sub + here, total, 0.0), axis=1, keepdims=True)
     inv = 1.0 / (col + prior)
-    for r in (2, 3, 1):
+    for r in (3, 1):
         along_y[r].wait_recv()
 
     def left(zz):
         rows = pl.ds(pl.multiple_of(zz * 64, 64), 64)
         v = acc[at(y, zz), LEFT]
-        for r in (1, 2, 3):
+        for r in (1, 3):
             v = v + yr[r, rows, :].astype(f32)
         return v
 
@@ -442,7 +450,7 @@
 def body(images, cents, tops):
     anyspec = pl.BlockSpec(memory_space=pl.ANY)
     vmem = pl.BlockSpec(memory_space=pltpu.VMEM)
-    ncopies = 96
+    ncopies = 108
     flops = 2 * 2 * (1024 * 4096 + 1024 * 1024) * D
     part, top = pl.pallas_call(
         kernel,
@@ -465,6 +473,8 @@
             pltpu.VMEM((512, D), bf16),
             pltpu.VMEM((4, 64, D // 2), bf16),
             pltpu.VMEM((4, 64, D // 2), bf16),
+            pltpu.VMEM((2, 64, D // 2), bf16),
+            pltpu.VMEM((2, 64, D // 2), bf16),
             pltpu.VMEM((4, 128, D // 2), bf16),
             pltpu.VMEM((4, 128, D // 2), bf16),
             pltpu.VMEM((4, 64, D // 2), bf16),

time: 101 us -> 94.1 us (0.932)
  Pallas kernels: 100 us -> 93.4 us
    pallas_call x1, Pallas kernels: 98.2 us -> 91.5 us  [body(): pl.pallas_call(kernel, out_shape=(jax.ShapeDtypeStruct((128, D), bf16), j...]
where the time goes in v3:
time: 94.1 us; the launch traced here: 94 us
  Pallas kernels  93.4 us (99%)
    pallas_call x1, Pallas kernels, body(): pl.pallas_call(kernel, out_shape=(jax.ShapeDtypeStruct((128, D), bf16), j...  91.5 us

profile of v3, /device:TPU:1, one launch (start us, length us, event | category | flops | bytes accessed | tf_op | source)
XLA Modules:
  0.0 94.0 jit_solution(1004376005555424721)
XLA Ops:
  0.6 91.5 %two_levels.1 = (bf16[128,1536]{1,0:T(8,128)(2,1)}, bf16[64,1536]{1,0:T(8,128)(2,1)}) custom-call(bf16[512,1536]{1,0:T(8,128)(2,1)} %images.1, bf16[1024,1536]{1,0:T(8,128)(2,1)} %cents.1, bf16[1024,1536]{1,0:T(8,128)(2,1)} %tops.1), custom_call_target="tpu_custom_call" | custom-call | flops 32212254720 | bytes 9437184 | tf_op jit(solution)/shard_map/two_levels/pallas_call | solution.py:455
  92.1 1.9 %hand_over.1 = (bf16[128,1536]{1,0:T(8,128)(2,1)}, bf16[1,64,1536]{2,1,0:T(8,128)(2,1)}) custom-call(bf16[128,1536]{1,0:T(8,128)(2,1)} %get-tuple-element.4.a, bf16[64,1536]{1,0:T(8,128)(2,1)} %get-tuple-element.5.b), custom_call_target="tpu_custom_call" | custom-call | tf_op jit(solution)/shard_map/hand_over/pallas_call | solution.py:504

commit v4 on v3

--- a/solution.py
+++ b/solution.py
@@ -14,6 +14,7 @@
 SHARD = 512
 ROWS = 1024
 HX, HQ = 128, 32
+LEFT_D = 640
 KAPPA = D ** -0.5 * 1.4426950408889634
 ORDER = (1, 3, 2)
 AT_X = {(0, 1): 1024, (0, 3): 1152, (0, 2): 2048, (1, 1): 2560, (1, 3): 3072, (1, 2): 3584}
@@ -227,11 +228,14 @@
             src_ref=buf.at[j, 0], dst_ref=buf.at[j, r], send_sem=ssem.at[j], recv_sem=rsem.at[j],
             device_id=peer(r), device_id_type=MESH) for r in range(1, count)]
 
-    def scores(sl, left, right, lo):
+    def dots(sl, left, right, lo):
         for n in range(2):
             cols = slice(n * 256, (n + 1) * 256)
             S[sl, :, cols] = lax.dot_general(
                 left[...], right[lo + n * 256:lo + (n + 1) * 256, :], NT, preferred_element_type=f32)
+
+    def scores(sl, left, right, lo):
+        dots(sl, left, right, lo)
         return soft(sl)
 
     def combine(buf, j, count):
@@ -270,8 +274,11 @@
             cp.start()
 
     def B(j):
+        wait_bytes(stat.at[j, pl.ds(1, 15)], sr.at[j])
+        weighted(j)
+
+    def weighted(j):
         at = CHUNKS[j]
-        wait_bytes(stat.at[j, pl.ds(1, 15)], sr.at[j])
         f = combine(stat, j, 16)
         for t in range(0, ROWS, 512):
             rows = slice(t, t + 512)
@@ -294,6 +301,9 @@
         if step[0] == "A":
             A(step[1])
         elif step[0] == "B":
+            if step[1] == 7:
+                for l in l_to:
+                    l.wait()
             B(step[1])
         else:
             arrive(*relay[step][0])
@@ -303,11 +313,7 @@
         rows = slice(t, t + 256)
         inv = 1.0 / (jnp.sum(mass[rows, :], axis=1, keepdims=True) + prior)
         data[rows, :] = ((acc[rows, :] + prior * ce[rows, :].astype(f32)) * inv).astype(bf16)
-    o1 = pltpu.make_async_copy(data.at[pl.ds(pl.multiple_of(di * 128, 128), 128)], out1, ld.at[0])
-    o1.start()
-
-    for l in l_to:
-        l.wait()
+
     mass[...] = jnp.zeros_like(mass)
     for h in range(2):
         m, l = scores(h, to, data, h * 512)
@@ -315,6 +321,8 @@
         stat2[h, 0, 1:2, :] = l
         for cp in stat_copies(stat2, h, 8, s2s, s2r, dppeer):
             cp.start()
+    o1 = pltpu.make_async_copy(data.at[pl.ds(pl.multiple_of(di * 128, 128), 128)], out1, ld.at[0])
+    o1.start()
     wait_bytes(stat2.at[0, pl.ds(1, 7)], s2r.at[0])
     f = combine(stat2, 0, 8)
     for t in range(0, ROWS, 512):
@@ -361,8 +369,12 @@
     def at(yy, zz):
         return pl.ds(pl.multiple_of(c * 512 + yy * 128 + zz * 64, 64), 64)
 
+    def total_of(yy, zz, cols):
+        rows = pl.ds(pl.multiple_of(yy * 128 + zz * 64, 64), 64)
+        return acc[at(yy, zz), cols] + drecv[rows, cols].astype(f32)
+
     zpartner = dev(x, y, zh, 1 - zl, c)
-    LEFT, RIGHT = slice(0, D // 2), slice(D // 2, D)
+    LEFT, RIGHT = slice(0, LEFT_D), slice(LEFT_D, D)
     first, along_y, along_z = {}, {}, {}
     for i in range(2):
         half = pl.multiple_of((1 - pair if i == 0 else pair) * 256, 256)
@@ -371,21 +383,20 @@
             cols = slice(d * 512, (d + 1) * 512)
             acc[src, cols] += lax.dot_general(Pb[src, :], data[512:1024, cols], NN, preferred_element_type=f32)
         d_copies[i].wait_recv()
-        acc[src, :] += drecv[pl.ds(half, 256), :].astype(f32)
         for r in ((2, 3) if i == 0 else (1, 0)):
             yy = xor4(y, r)
-            zs[r] = acc[at(yy, 1 - zl), RIGHT].astype(bf16)
+            zs[r] = total_of(yy, 1 - zl, RIGHT).astype(bf16)
             along_z[r] = send(r, zs.at[r], zr.at[r], zpartner)
             if r == 2:
                 for h in range(2):
-                    fs[h] = acc[at(yy, h), LEFT].astype(bf16)
+                    fs[h] = total_of(yy, h, LEFT).astype(bf16)
                     first[h] = send(4 + 2 * h, fs.at[h], fr.at[h], dev(x, xor4(y, 1 + 2 * h), zh, zl, c))
     for r in (3, 1):
         yy = xor4(y, r)
         h = 0 if r == 3 else 1
         first[h].wait_recv()
         for zz in range(2):
-            v = acc[at(yy, zz), LEFT]
+            v = total_of(yy, zz, LEFT)
             if zz == h:
                 v = v + fr[h].astype(f32)
             ys[r, zz * 64:(zz + 1) * 64, :] = v.astype(bf16)
@@ -394,7 +405,7 @@
     for r in (2, 3, 1):
         yy = xor4(y, r)
         along_z[r].wait_recv()
-        y2s[r] = (acc[at(yy, zl), RIGHT] + zr[r].astype(f32)).astype(bf16)
+        y2s[r] = (total_of(yy, zl, RIGHT) + zr[r].astype(f32)).astype(bf16)
         along_y2[r] = send(8 + r, y2s.at[r], y2r.at[r], dev(x, yy, zh, zl, c))
     here = c * 512 + y * 128 + zl * 64
     wait_bytes(msum.at[pl.ds(1, 15)], msr)
@@ -410,7 +421,7 @@
 
     def left(zz):
         rows = pl.ds(pl.multiple_of(zz * 64, 64), 64)
-        v = acc[at(y, zz), LEFT]
+        v = total_of(y, zz, LEFT)
         for r in (1, 3):
             v = v + yr[r, rows, :].astype(f32)
         return v
@@ -419,7 +430,7 @@
     along_z2 = send(12, z2s, z2r, zpartner)
     own = left(zl) + prior * to[at(y, zl), LEFT].astype(f32)
     along_z[0].wait_recv()
-    right = acc[at(y, zl), RIGHT] + prior * to[at(y, zl), RIGHT].astype(f32) + zr[0].astype(f32)
+    right = total_of(y, zl, RIGHT) + prior * to[at(y, zl), RIGHT].astype(f32) + zr[0].astype(f32)
     for r in (2, 3, 1):
         along_y2[r].wait_recv()
         right = right + y2r[r].astype(f32)
@@ -471,16 +482,16 @@
             pltpu.VMEM((16, 1, 1024), f32),
             pltpu.VMEM((512, D), bf16),
             pltpu.VMEM((512, D), bf16),
-            pltpu.VMEM((4, 64, D // 2), bf16),
-            pltpu.VMEM((4, 64, D // 2), bf16),
-            pltpu.VMEM((2, 64, D // 2), bf16),
-            pltpu.VMEM((2, 64, D // 2), bf16),
-            pltpu.VMEM((4, 128, D // 2), bf16),
-            pltpu.VMEM((4, 128, D // 2), bf16),
-            pltpu.VMEM((4, 64, D // 2), bf16),
-            pltpu.VMEM((4, 64, D // 2), bf16),
-            pltpu.VMEM((64, D // 2), bf16),
-            pltpu.VMEM((64, D // 2), bf16),
+            pltpu.VMEM((4, 64, D - LEFT_D), bf16),
+            pltpu.VMEM((4, 64, D - LEFT_D), bf16),
+            pltpu.VMEM((2, 64, LEFT_D), bf16),
+            pltpu.VMEM((2, 64, LEFT_D), bf16),
+            pltpu.VMEM((4, 128, LEFT_D), bf16),
+            pltpu.VMEM((4, 128, LEFT_D), bf16),
+            pltpu.VMEM((4, 64, D - LEFT_D), bf16),
+            pltpu.VMEM((4, 64, D - LEFT_D), bf16),
+            pltpu.VMEM((64, LEFT_D), bf16),
+            pltpu.VMEM((64, LEFT_D), bf16),
             pltpu.VMEM((64, D), bf16),
             pltpu.SemaphoreType.DMA((ncopies,)),
             pltpu.SemaphoreType.DMA((ncopies,)),

time: 94.1 us -> 93.6 us (level)
  no operation moved by 1% of the time
where the time goes in v4:
time: 93.6 us; the launch traced here: 93.5 us
  Pallas kernels  92.9 us (99%)
    pallas_call x1, Pallas kernels, body(): pl.pallas_call(kernel, out_shape=(jax.ShapeDtypeStruct((128, D), bf16), j...  91 us
    pallas_call x1, Pallas kernels, body(): pl.pallas_call(hand_over, out_shape=(jax.ShapeDtypeStruct((128, D), bf16)...  1.88 us

profile of v4, /device:TPU:1, one launch (start us, length us, event | category | flops | bytes accessed | tf_op | source)
XLA Modules:
  0.0 93.5 jit_solution(15048795227148009218)
XLA Ops:
  0.6 91.0 %two_levels.1 = (bf16[128,1536]{1,0:T(8,128)(2,1)}, bf16[64,1536]{1,0:T(8,128)(2,1)}) custom-call(bf16[512,1536]{1,0:T(8,128)(2,1)} %images.1, bf16[1024,1536]{1,0:T(8,128)(2,1)} %cents.1, bf16[1024,1536]{1,0:T(8,128)(2,1)} %tops.1), custom_call_target="tpu_custom_call" | custom-call | flops 32212254720 | bytes 9437184 | tf_op jit(solution)/shard_map/two_levels/pallas_call | solution.py:466
  91.6 1.9 %hand_over.1 = (bf16[128,1536]{1,0:T(8,128)(2,1)}, bf16[1,64,1536]{2,1,0:T(8,128)(2,1)}) custom-call(bf16[128,1536]{1,0:T(8,128)(2,1)} %get-tuple-element.4.a, bf16[64,1536]{1,0:T(8,128)(2,1)} %get-tuple-element.5.b), custom_call_target="tpu_custom_call" | custom-call | tf_op jit(solution)/shard_map/hand_over/pallas_call | solution.py:515
